TPU v7x, 512 devices: a whole 4x4x16 slice. The times are simulated.
512 devices in a mesh: dp: 32 (over z_hi, x, core), tensor: 16 (over y, z_lo).
Axes of the slice: x: 4, y: 4, z: 16 (z_hi: 4, z_lo: 4; z = z_hi * 4 + z_lo), core: 2. Of those that a mesh axis runs over, the one named last changes fastest.
Arguments:
- weight: bfloat16 [16384, 4096], P('tensor', 'dp'), may hold values from -0.046875 to 0.046875
- inputs: bfloat16 [16384, 16384], P('dp', 'tensor'), may hold values from -6 to 6
- cotangent: bfloat16 [16384, 4096], P('dp', 'tensor'), may hold values from -30 to 30
- projector: bfloat16 [16384, 1024], P('tensor'), may hold values from -0.046875 to 0.046875
- first_moment: float32 [1024, 4096], P('dp', 'tensor'), may hold values from -18 to 18
- second_moment: float32 [1024, 4096], P('dp', 'tensor'), may hold values from 0.2 to 2
Outputs:
- new_weight: bfloat16 [16384, 4096], P('tensor', 'dp')
- new_first: float32 [1024, 4096], P('dp', 'tensor')
- new_second: float32 [1024, 4096], P('dp', 'tensor')
All inputs are finite; a program needn't handle non-finite values.
Results may differ from a plain program's by a relative error of at most 0.0053.
Values may be sent and summed in bfloat16 or wider, within the bound.
A program may use at most 64 MiB of HBM per device.

v0:
```python
import jax
import jax.numpy as jnp
from jax import lax
from jax.sharding import PartitionSpec as P

STEP = 10


def local(weight, inputs, cotangent, projector, first_moment, second_moment):
    partial_proj = jnp.dot(inputs, projector, preferred_element_type=jnp.float32)
    projected = lax.psum(partial_proj, "tensor").astype(jnp.bfloat16)
    partial_low = lax.dot_general(
        projected, cotangent, (((0,), (0,)), ((), ())), preferred_element_type=jnp.float32
    )
    low = lax.psum_scatter(partial_low, "dp", scatter_dimension=0, tiled=True) / lax.axis_size("dp")
    new_first = 0.9 * first_moment + 0.1 * low
    new_second = 0.999 * second_moment + 0.001 * low * low
    first_hat = new_first / (1.0 - 0.9**STEP)
    second_hat = new_second / (1.0 - 0.999**STEP)
    update = (first_hat / (jnp.sqrt(second_hat) + 1e-08)).astype(jnp.bfloat16)
    group_rows = lax.all_gather(update, "tensor", axis=1, tiled=True)
    width = weight.shape[1]
    col_start = lax.axis_index("dp") * width
    needed = lax.dynamic_slice_in_dim(
        lax.all_gather(group_rows, "dp", axis=0, tiled=True), col_start, width, 1
    )
    change = jnp.dot(projector, needed, preferred_element_type=jnp.float32)
    new_weight = (weight.astype(jnp.float32) - 0.5 * change).astype(jnp.bfloat16)
    return (new_weight, new_first, new_second)


def solution(mesh):
    placed = (
        P("tensor", "dp"),
        P("dp", "tensor"),
        P("dp", "tensor"),
        P("tensor", None),
        P("dp", "tensor"),
        P("dp", "tensor"),
    )
    return jax.shard_map(
        local,
        mesh=mesh,
        in_specs=placed,
        out_specs=(P("tensor", "dp"), P("dp", "tensor"), P("dp", "tensor")),
        check_vma=False,
    )
```

profile of v0, /device:TPU:1, one launch (start us, length us, event | category | flops | bytes accessed | tf_op | source)
XLA Modules:
  0.0 425.1 jit_solution(5828041688200153356)
XLA Ops:
  7.2 0.0 copy-start
  7.2 0.0 reduce-scatter.2.cloned.1.call-start
  7.2 1.5 copy-done
  8.8 3.8 fusion.7
  12.6 0.0 copy-start.1
  12.6 100.7 %all-reduce.1 = bf16[512,1024]{1,0:T(8,128)(2,1)S(1)} all-reduce(f32[512,1024]{1,0:T(8,128)} %fusion.7), channel_id=1, replica_groups=mesh['dp'=32,'tensor'=16] {'tensor'}, use_global_device_ids=true, to_apply=%region_0.0 | all-reduce | flops 524288 | bytes 3145728 | tf_op jit(solution)/shard_map/psum | solution.py:11
  113.3 0.0 copy-done.1
  113.3 0.0 copy-start.2
  113.3 0.0 copy-start.3
  113.3 1.4 fusion.8
  114.8 0.0 reduce-scatter.2.cloned.1.call-update
  114.8 0.0 all-gather.2.cloned.1.call-start
  114.8 123.9 %reduce-scatter.2.cloned.1.call-done = f32[32,256]{1,0:T(8,128)} async-done(((f32[1024,256]{1,0:T(8,128)}), f32[32,256]{1,0:T(8,128)}) %reduce-scatter.2.cloned.1.call-update) | async-done | bytes 32784 | tf_op jit(solution)/shard_map/reduce_scatter | solution.py:15
  238.7 0.0 copy-done.2
  238.7 0.0 copy-done.3
  238.7 1.4 divide_convert_fusion
  240.1 37.0 %all_gather.6 = bf16[32,4096]{1,0:T(8,128)(2,1)} all-gather(bf16[32,256]{1,0:T(8,128)(2,1)S(1)} %get-tuple-element.6), channel_id=1, replica_groups=mesh['dp'=32,'tensor'=16] {'tensor'}, dimensions={1}, use_global_device_ids=true | all-gather | bytes 278528 | tf_op jit(solution)/shard_map/all_gather | solution.py:21
  277.1 0.0 all-gather.2.cloned.1.call-update
  277.2 1.1 copy.9
  278.3 137.4 %all-gather.2.cloned.1.call-done = bf16[1024,4096]{1,0:T(8,128)(2,1)} async-done(((bf16[32,4096]{1,0:T(8,128)(2,1)}), bf16[1024,4096]{1,0:T(8,128)(2,1)}) %all-gather.2.cloned.1.call-update) | async-done | bytes 8388624 | tf_op jit(solution)/shard_map/all_gather | solution.py:25
  415.6 1.8 fusion.2
  417.4 0.8 copy.10
Async XLA Ops:
  7.2 1.6 copy-start
  7.2 231.6 %reduce-scatter.2.cloned.1.call-start = ((), (), s32[]{:S(2)}) async-start(), calls=%async_computation.1 | async-start | bytes 1081344 | tf_op jit(solution)/shard_map/reduce_scatter | solution.py:15
  12.6 100.7 %copy-start.1 = (bf16[512,256]{1,0:T(8,128)(2,1)S(1)}, bf16[512,256]{1,0:T(8,128)(2,1)}, u32[]{:S(2)}) copy-start(bf16[512,256]{1,0:T(8,128)(2,1)} %param.8) | copy-start | bytes 786436
  113.3 125.4 %copy-start.2 = (f32[32,256]{1,0:T(8,128)S(1)}, f32[32,256]{1,0:T(8,128)}, u32[]{:S(2)}) copy-start(f32[32,256]{1,0:T(8,128)} %param.10) | copy-start | bytes 98308
  113.3 125.4 %copy-start.3 = (f32[32,256]{1,0:T(8,128)S(1)}, f32[32,256]{1,0:T(8,128)}, u32[]{:S(2)}) copy-start(f32[32,256]{1,0:T(8,128)} %param.11) | copy-start | bytes 98308
  114.8 300.8 %all-gather.2.cloned.1.call-start = ((), (), s32[]{:S(2)}) async-start(), calls=%async_computation.2 | async-start | bytes 8650752 | tf_op jit(solution)/shard_map/all_gather | solution.py:25
Sparse Core Ops, SparseCore 0:
  114.9 123.7 reduce-scatter.1
  277.3 138.3 all-gather.1
where the time goes:
time: 425 us
  waiting for transfers between devices  261 us (61%)
  blocking collectives  138 us (32%)
  between operations  14.1 us (3%)
  matrix products  7.04 us (2%)
    all_gather x1, waiting for transfers between devices, local(): lax.all_gather(group_rows, 'dp', axis=0, tiled=True)  137 us
    reduce_scatter x1, waiting for transfers between devices, local(): lax.psum_scatter(partial_low, 'dp', scatter_dimension=0, tiled=True)  124 us
    psum x1, blocking collectives, local(): projected = lax.psum(partial_proj, 'tensor').astype(jnp.bfloat16)  101 us
    all_gather x1, blocking collectives, local(): group_rows = lax.all_gather(update, 'tensor', axis=1, tiled=True)  37 us
  transfers between devices with their start and end apart: 2, of which 2 were waited for; matrix products, arithmetic and copies ran while one was open for 0% of the time, Pallas kernels for 0%

commit v1 on v0

v1 whole, which is shorter than its diff:
```python
import jax
import jax.numpy as jnp
from jax import lax
from jax.experimental import pallas as pl
from jax.experimental.pallas import tpu as pltpu
from jax.sharding import PartitionSpec as P

STEP = 10
REPLICAS = 32
MESH = pl.DeviceIdType.MESH
F32, BF16 = jnp.float32, jnp.bfloat16


def kernel(
    w_hbm, x_hbm, ct_hbm, p_hbm, m1_hbm, m2_hbm,
    ow, o1, o2,
    w_v, x_v, ct_v, p_v, m1_v, m2_v,
    part, y1s, y1r, y2s, y2r, ysum, zs, zr, proj,
    plow, cs, cr, csum, xs, xr, xsum, hs, hr, upd, need, acc,
    lsem, ssem, rsem,
):
    dp, t = lax.axis_index("dp"), lax.axis_index("tensor")
    zh, x, c = lax.div(dp, 8), lax.rem(lax.div(dp, 2), 4), lax.rem(dp, 2)
    y, zl = lax.div(t, 4), lax.rem(t, 4)
    xh, xx = lax.div(x, 2), lax.rem(x, 2)
    zlh = lax.div(zl, 2)
    plus = lambda v, k: lax.rem(v + k, 4)
    yp, y2, ym = plus(y, 1), plus(y, 2), plus(y, 3)
    other = 1 - c

    def dev(zh_=zh, x_=x, c_=c, y_=y, zl_=zl):
        return {"dp": zh_ * 8 + x_ * 2 + c_, "tensor": y_ * 4 + zl_}

    y_up, y_down = dev(y_=yp), dev(y_=ym)
    moved = (zh != y) | (x != zl)
    across = [dev(y, zl, c, zh, x), dev(y, zl, other, zh, x)]

    count = {"l": 0, "r": 0}

    def load(src, dst):
        copy = pltpu.make_async_copy(src, dst, lsem.at[count["l"]])
        count["l"] += 1
        copy.start()
        return copy

    barrier = pltpu.get_barrier_semaphore()
    partners = [y_up, y_down, dev(c_=other)]
    partners += [dev(zl_=plus(zl, k)) for k in (1, 2, 3)]
    partners += [dev(x_=plus(x, k)) for k in (1, 2, 3)]
    partners += [dev(zh_=plus(zh, k)) for k in (1, 2, 3)]

    def signal(device):
        pl.semaphore_signal(barrier, inc=1, device_id=device, device_id_type=MESH)

    for device in partners:
        signal(device)

    @pl.when(moved)
    def _():
        signal(across[0])
        signal(across[1])

    x_load = [load(x_hbm.at[pl.ds(y2 * 128, 128)], x_v.at[y2])]
    p_load = []
    for s in range(4):
        h, q = divmod(s, 2)
        pair = []
        for i in range(2):
            col = (2 * q + i) * 256 + h * 128
            pair.append(load(p_hbm.at[:, pl.ds(col, 128)], p_v.at[s, :, pl.ds(i * 128, 128)]))
        p_load.append(pair)
        if s == 0:
            for b in (yp, ym, y):
                x_load.append(load(x_hbm.at[pl.ds(b * 128, 128)], x_v.at[b]))
    ct_load = load(ct_hbm, ct_v)
    m_load = [load(m1_hbm, m1_v), load(m2_hbm, m2_v)]
    w_load = load(w_hbm, w_v)

    sends = []

    def copy_of(src, dst, device, index):
        return pltpu.make_async_remote_copy(
            src_ref=src, dst_ref=dst, send_sem=ssem.at[index], recv_sem=rsem.at[index],
            device_id=device, device_id_type=MESH,
        )

    def new():
        count["r"] += 1
        return count["r"] - 1

    def send(src, dst, device, index):
        copy = copy_of(src, dst, device, index)
        copy.start()
        sends.append(copy)

    def arrived(dst, index):
        copy_of(dst, dst, y_up, index).wait_recv()

    ids = {}

    def sem(*key):
        if key not in ids:
            ids[key] = new()
        return ids[key]

    def dot(a, b):
        return jnp.dot(a, b, preferred_element_type=F32)

    def rows(b, n=4):
        return pl.ds(b * 4, n)

    def project(s, b):
        part[s, rows(b)] = dot(x_v[b], p_v[s]).reshape(4, 32, 256)

    def a0(s):
        for copy in p_load[s]:
            copy.wait()
        if s == 0:
            x_load[0].wait()
        project(s, y2)
        y1s[s] = part[s, rows(y2)].astype(BF16)
        if s == 0:

            @pl.when(moved)
            def _():
                pl.semaphore_wait(barrier, 14)

            @pl.when(jnp.logical_not(moved))
            def _():
                pl.semaphore_wait(barrier, 12)

        send(y1s.at[s, pl.ds(0, 2)], y1r.at[s, 0], y_up, sem("y1u", s))
        send(y1s.at[s, pl.ds(2, 2)], y1r.at[s, 1], y_down, sem("y1d", s))
        if s == 0:
            for copy in x_load[1:]:
                copy.wait()


        project(s, yp)
        project(s, ym)
        project(s, y)

    def a1(s):
        up, down = part[s, rows(yp)], part[s, rows(ym)]
        arrived(y1r.at[s, 0], sem("y1u", s))
        y2s[s, 0, 0:2] = (up[0:2] + y1r[s, 0].astype(F32)).astype(BF16)
        y2s[s, 0, 2:4] = up[2:4].astype(BF16)
        send(y2s.at[s, 0], y2r.at[s, 0], y_up, sem("y2u", s))
        arrived(y1r.at[s, 1], sem("y1d", s))
        y2s[s, 1, 0:2] = down[0:2].astype(BF16)
        y2s[s, 1, 2:4] = (down[2:4] + y1r[s, 1].astype(F32)).astype(BF16)
        send(y2s.at[s, 1], y2r.at[s, 1], y_down, sem("y2d", s))

    def a2(s):
        arrived(y2r.at[s, 0], sem("y2u", s))
        arrived(y2r.at[s, 1], sem("y2d", s))
        total = part[s, rows(y)] + y2r[s, 0].astype(F32) + y2r[s, 1].astype(F32)
        ysum[s] = total
        zs[s] = total.astype(BF16)
        for k in (2, 1, 3):
            to = plus(zl, k)
            send(zs.at[s, to], zr.at[s, k - 1], dev(zl_=to), sem("z", s, k))

    def a3(s):
        total = ysum[s, zl]
        for k in (1, 2, 3):
            arrived(zr.at[s, k - 1], sem("z", s, k))
            total = total + zr[s, k - 1].astype(F32)
        proj[s, t] = total.astype(BF16)
        for k in (2, 1, 3):
            send(proj.at[s, t], proj.at[s, t], dev(zl_=plus(zl, k)), sem("za", s, k))

    def a4(s):
        for k in (1, 2, 3):
            arrived(proj.at[s, y * 4 + plus(zl, 4 - k)], sem("za", s, k))
        mine = proj.at[s, rows(y)]
        send(mine, mine, y_up, sem("ya1u", s))
        send(mine, mine, y_down, sem("ya1d", s))

    def a5(s):
        arrived(proj.at[s, rows(ym)], sem("ya1u", s))
        first = proj.at[s, rows(ym, 2)]
        send(first, first, y_up, sem("ya2u", s))
        arrived(proj.at[s, rows(yp)], sem("ya1d", s))
        second = proj.at[s, pl.ds(yp * 4 + 2, 2)]
        send(second, second, y_down, sem("ya2d", s))

    def a6(s):
        h, q = divmod(s, 2)
        arrived(proj.at[s, rows(y2, 2)], sem("ya2u", s))
        arrived(proj.at[s, pl.ds(y2 * 4 + 2, 2)], sem("ya2d", s))
        if s == 0:
            ct_load.wait()
        block = lax.dot_general(
            proj[s].reshape(512, 256), ct_v[...], (((0,), (0,)), ((), ())), preferred_element_type=F32
        ).reshape(2, 2, 2, 32, 256)
        for zz in range(2):
            for i in range(2):
                for cc in range(2):
                    plow[h, cc, i, 2 * q + zz] = block[zz, i, cc]
        if q == 1:
            cs[h] = plow[h, other].astype(BF16)
            send(cs.at[h], cr.at[h], dev(c_=other), sem("c", h))

    def b0(h):
        arrived(cr.at[h], sem("c", h))
        total = plow[h, c] + cr[h].astype(F32)
        csum[h] = total
        xs[h] = total.astype(BF16)
        for k in (2, 1, 3):
            to = plus(x, k)
            index = sem("x", k)

            @pl.when(lax.div(to, 2) == h)
            def _():
                copy_of(xs.at[h, lax.rem(to, 2)], xr.at[k - 1], dev(x_=to), index).start()

    def b1(h):
        for k in (1, 2, 3):
            sem("h", k)

        @pl.when(xh == h)
        def _():
            total = csum[h, xx]
            for k in (1, 2, 3):
                arrived(xr.at[k - 1], sem("x", k))
                total = total + xr[k - 1].astype(F32)
            xsum[...] = total
            hs[...] = total.astype(BF16)
            for k in (2, 1, 3):
                to = plus(zh, k)
                copy_of(hs.at[to], hr.at[k - 1], dev(zh_=to), sem("h", k)).start()

    def b2(h):
        for k in (0, 1):
            sem("t", k)
        if h == 0:
            for copy in m_load:
                copy.wait()

        @pl.when(xh == h)
        def _():
            total = xsum[zh]
            for k in (1, 2, 3):
                arrived(hr.at[k - 1], sem("h", k))
                total = total + hr[k - 1].astype(F32)
            low = total / REPLICAS
            first = 0.9 * m1_v[...] + 0.1 * low
            second = 0.999 * m2_v[...] + 0.001 * low * low
            o1[...] = first
            o2[...] = second
            first_hat = first / (1.0 - 0.9**STEP)
            second_hat = second / (1.0 - 0.999**STEP)
            update = (first_hat / (jnp.sqrt(second_hat) + 1e-08)).astype(BF16)
            upd[0] = update[:, :128]
            upd[1] = update[:, 128:]

            @pl.when(moved)
            def _():
                copy_of(upd.at[c], need.at[dp], across[0], sem("t", 0)).start()

            @pl.when(jnp.logical_not(moved))
            def _():
                pltpu.make_async_copy(upd.at[c], need.at[dp], rsem.at[sem("t", 0)]).start()

            copy_of(upd.at[other], need.at[dp], across[1], sem("t", 1)).start()

    def c0(h):
        for k in (1, 2, 3):
            sem("n", k)

        @pl.when(zlh == h)
        def _():
            arrived(need.at[t * 2 + c], sem("t", 0))
            arrived(need.at[t * 2 + other], sem("t", 1))
            mine = need.at[pl.ds(t * 2, 2)]
            for k in (2, 1, 3):
                copy_of(mine, mine, dev(zl_=plus(zl, k)), sem("n", k)).start()

    def c1(h):
        for k in (1, 2, 3):
            source = plus(zl, 4 - k)

            @pl.when(lax.div(source, 2) == h)
            def _():
                arrived(need.at[pl.ds((y * 4 + source) * 2, 2)], sem("n", k))

        mine = need.at[pl.ds(y * 8 + h * 4, 4)]
        send(mine, mine, y_up, sem("n1u", h))
        send(mine, mine, y_down, sem("n1d", h))

    def c2(h):
        arrived(need.at[pl.ds(ym * 8 + h * 4, 4)], sem("n1u", h))
        first = need.at[pl.ds(ym * 8 + h * 4, 2)]
        send(first, first, y_up, sem("n2u", h))
        arrived(need.at[pl.ds(yp * 8 + h * 4, 4)], sem("n1d", h))
        second = need.at[pl.ds(yp * 8 + h * 4 + 2, 2)]
        send(second, second, y_down, sem("n2d", h))

    def d(h):
        arrived(need.at[pl.ds(y2 * 8 + h * 4, 2)], sem("n2u", h))
        arrived(need.at[pl.ds(y2 * 8 + h * 4 + 2, 2)], sem("n2d", h))
        lower = [need[zz * 8 + h * 4 : zz * 8 + h * 4 + 4].reshape(128, 128) for zz in range(4)]
        left = jnp.concatenate(lower[:2], axis=0)
        right = jnp.concatenate(lower[2:], axis=0)
        for r in range(0, 1024, 256):
            span = slice(r, r + 256)
            change = dot(p_v[2 * h, span], left) + dot(p_v[2 * h + 1, span], right)
            if h == 0:
                acc[span] = change
            else:
                ow[span] = (w_v[span].astype(F32) - 0.5 * (acc[span] + change)).astype(BF16)

    plan = []
    for s in range(4):
        for j, stage in enumerate((a0, a1, a2, a3, a4, a5, a6)):
            plan.append((s + j, 0, -j, stage, s))
    for h in range(2):
        for j, stage in enumerate((b0, b1, b2, c0, c1, c2, d)):
            plan.append((8 + 2 * h + j, 1, -j, stage, h))
    for tick, _, _, stage, index in sorted(plan, key=lambda e: e[:3]):
        stage(index)
        if stage is b2 and index == 1:
            w_load.wait()

    for copy in sends:
        copy.wait_send()
    for k in (1, 2, 3):
        copy_of(xs.at[0, 0], xr.at[k - 1], y_up, sem("x", k)).wait_send()
        copy_of(hs.at[0], hr.at[k - 1], y_up, sem("h", k)).wait_send()
        copy_of(need.at[pl.ds(0, 2)], need.at[pl.ds(0, 2)], y_up, sem("n", k)).wait_send()

    @pl.when(moved)
    def _():
        copy_of(upd.at[0], need.at[0], y_up, sem("t", 0)).wait_send()

    copy_of(upd.at[0], need.at[0], y_up, sem("t", 1)).wait_send()


def local(weight, inputs, cotangent, projector, first_moment, second_moment):
    v = pltpu.VMEM
    return pl.pallas_call(
        kernel,
        out_shape=(
            jax.ShapeDtypeStruct((1024, 128), BF16),
            jax.ShapeDtypeStruct((32, 256), F32),
            jax.ShapeDtypeStruct((32, 256), F32),
        ),
        in_specs=[pl.BlockSpec(memory_space=pl.ANY)] * 6,
        out_specs=[pl.BlockSpec(memory_space=pltpu.VMEM)] * 3,
        scratch_shapes=[
            v((1024, 128), BF16),
            v((4, 128, 1024), BF16),
            v((512, 256), BF16),
            v((4, 1024, 256), BF16),
            v((32, 256), F32),
            v((32, 256), F32),
            v((4, 16, 32, 256), F32),
            v((4, 4, 32, 256), BF16),
            v((4, 2, 2, 32, 256), BF16),
            v((4, 2, 4, 32, 256), BF16),
            v((4, 2, 4, 32, 256), BF16),
            v((4, 4, 32, 256), F32),
            v((4, 4, 32, 256), BF16),
            v((4, 3, 32, 256), BF16),
            v((4, 16, 32, 256), BF16),
            v((2, 2, 2, 4, 32, 256), F32),
            v((2, 2, 4, 32, 256), BF16),
            v((2, 2, 4, 32, 256), BF16),
            v((2, 2, 4, 32, 256), F32),
            v((2, 2, 4, 32, 256), BF16),
            v((3, 4, 32, 256), BF16),
            v((4, 32, 256), F32),
            v((4, 32, 256), BF16),
            v((3, 32, 256), BF16),
            v((2, 32, 128), BF16),
            v((32, 32, 128), BF16),
            v((1024, 128), F32),
            pltpu.SemaphoreType.DMA((20,)),
            pltpu.SemaphoreType.DMA((96,)),
            pltpu.SemaphoreType.DMA((96,)),
        ],
        compiler_params=pltpu.CompilerParams(
            collective_id=0, has_side_effects=True, vmem_limit_bytes=40 * 2**20
        ),
    )(weight, inputs, cotangent, projector, first_moment, second_moment)


def solution(mesh):
    placed = (
        P("tensor", "dp"),
        P("dp", "tensor"),
        P("dp", "tensor"),
        P("tensor", None),
        P("dp", "tensor"),
        P("dp", "tensor"),
    )
    return jax.shard_map(
        local,
        mesh=mesh,
        in_specs=placed,
        out_specs=(P("tensor", "dp"), P("dp", "tensor"), P("dp", "tensor")),
        check_vma=False,
    )
```

time: 425 us -> 105 us (0.25)
  waiting for transfers between devices: 261 us -> 0 us
  blocking collectives: 138 us -> 0 us
  Pallas kernels: 0 us -> 94.3 us
  between operations: 14.1 us -> 0.65 us
  matrix products: 7.04 us -> 0 us
  local copies, waits for them, and re-layouts: 3.49 us -> 8.16 us
    all_gather x1 -> x0, waiting for transfers between devices: 137 us -> none  [local(): lax.all_gather(group_rows, 'dp', axis=0, tiled=True)]
    reduce_scatter x1 -> x0, waiting for transfers between devices: 124 us -> none  [local(): lax.psum_scatter(partial_low, 'dp', scatter_dimension=0, tiled=True)]
    psum x1 -> x0, blocking collectives: 101 us -> none  [local(): projected = lax.psum(partial_proj, 'tensor').astype(jnp.bfloat16)]
    pallas_call x0 -> x1, Pallas kernels: none -> 94.3 us  [local(): pl.pallas_call(kernel, out_shape=(jax.ShapeDtypeStruct((1024, 128), BF16)...]
    all_gather x1 -> x0, blocking collectives: 37 us -> none  [local(): group_rows = lax.all_gather(update, 'tensor', axis=1, tiled=True)]
    dot_general x3 -> x0, matrix products: 7.04 us -> none  [the longest x1 3.82 us: local(): jnp.dot(inputs, projector, preferred_element_type=jnp.float32)]
    unnamed x10 -> x15, local copies, waits for them, and re-layouts: 3.49 us -> 8.16 us
  transfers between devices with their start and end apart: 2 -> 0, of which waited for: 2 -> 0; matrix products, arithmetic and copies ran while one was open for 0% -> 0% of each run, Pallas kernels for 0% -> 0%
where the time goes in v1:
time: 105 us; the launch traced here: 103 us
  Pallas kernels  94.3 us (90%)
  local copies, waits for them, and re-layouts  8.16 us (8%)
    pallas_call x1, Pallas kernels, local(): pl.pallas_call(kernel, out_shape=(jax.ShapeDtypeStruct((1024, 128), BF16)...  94.3 us
    unnamed x15, local copies, waits for them, and re-layouts  8.16 us

profile of v1, /device:TPU:1, one launch (start us, length us, event | category | flops | bytes accessed | tf_op | source)
XLA Modules:
  0.0 103.2 jit_solution(17663805135218715645)
XLA Ops:
  0.6 0.0 copy-start
  0.6 1.6 %copy-done = bf16[1024,1024]{1,0:T(8,128)(2,1)S(1)} copy-done((bf16[1024,1024]{1,0:T(8,128)(2,1)S(1)}, bf16[1024,1024]{1,0:T(8,128)(2,1)}, u32[]{:S(2)}) %copy-start) | copy-done | bytes 2097176
  2.2 0.0 copy-start.1
  2.2 1.2 %copy-done.1 = bf16[512,1024]{1,0:T(8,128)(2,1)S(1)} copy-done((bf16[512,1024]{1,0:T(8,128)(2,1)S(1)}, bf16[512,1024]{1,0:T(8,128)(2,1)}, u32[]{:S(2)}) %copy-start.1) | copy-done | bytes 1048600
  3.4 0.0 copy-start.2
  3.5 0.9 copy-done.2
  4.4 0.0 copy-start.3
  4.4 0.9 copy-done.3
  5.4 0.0 copy-start.4
  5.4 0.8 copy-done.4
  6.1 0.0 copy-start.5
  6.1 0.8 copy-done.5
  6.9 94.3 %shard_map.85 = (bf16[1024,128]{1,0:T(8,128)(2,1)S(1)}, f32[32,256]{1,0:T(8,128)S(1)}, f32[32,256]{1,0:T(8,128)S(1)}) custom-call(bf16[1024,128]{1,0:T(8,128)(2,1)S(1)} %copy-done.2, bf16[512,1024]{1,0:T(8,128)(2,1)S(1)} %copy-done.1, bf16[512,256]{1,0:T(8,128)(2,1)S(1)} %copy-done.3, bf16[1024,1024]{1,0:T(8,128)(2,1)S(1)} %copy-done, ...), custom_call_target="tpu_custom_call" | custom-call | tf_op jit(solution)/shard_map/pallas_call | solution.py:342
  101.2 0.7 copy.12
  101.9 0.6 copy.13
  102.5 0.6 copy.14
Async XLA Ops:
  0.6 1.6 %copy-start = (bf16[1024,1024]{1,0:T(8,128)(2,1)S(1)}, bf16[1024,1024]{1,0:T(8,128)(2,1)}, u32[]{:S(2)}) copy-start(bf16[1024,1024]{1,0:T(8,128)(2,1)} %p_hbm.1) | copy-start | bytes 6291460
  2.2 1.2 %copy-start.1 = (bf16[512,1024]{1,0:T(8,128)(2,1)S(1)}, bf16[512,1024]{1,0:T(8,128)(2,1)}, u32[]{:S(2)}) copy-start(bf16[512,1024]{1,0:T(8,128)(2,1)} %x_hbm.1) | copy-start | bytes 3145732
  3.4 0.9 copy-start.2
  4.4 0.9 copy-start.3
  5.4 0.8 copy-start.4
  6.1 0.8 copy-start.5

commit v2 on v0

v2 whole, which is shorter than its diff:
```python
import jax
import jax.numpy as jnp
from jax import lax
from jax.experimental import pallas as pl
from jax.experimental.pallas import tpu as pltpu
from jax.sharding import PartitionSpec as P

STEP = 10
REPLICAS = 32
MESH = pl.DeviceIdType.MESH
F32, BF16 = jnp.float32, jnp.bfloat16


def kernel(
    w_hbm, x_hbm, ct_hbm, p_hbm, m1_hbm, m2_hbm,
    ow, o1, o2,
    w_v, x_v, ct_v, p_v, m_v, mr_v,
    ys, yr, yown, zs, zr, proj,
    plow, cs, cr, csum, xs, xr, xsum, hs, hr, low_v, back, upd, need, acc,
    lsem, ssem, rsem,
):
    dp, t = lax.axis_index("dp"), lax.axis_index("tensor")
    zh, x, c = lax.div(dp, 8), lax.rem(lax.div(dp, 2), 4), lax.rem(dp, 2)
    y, zl = lax.div(t, 4), lax.rem(t, 4)
    xh, xx = lax.div(x, 2), lax.rem(x, 2)
    other = 1 - c
    moved = zh != y
    apart = x != zl

    def plus(v, k):
        return lax.rem(v + k, 4)

    def dev(zh_=zh, x_=x, c_=c, y_=y, zl_=zl):
        return {"dp": zh_ * 8 + x_ * 2 + c_, "tensor": y_ * 4 + zl_}

    count = {"l": 0}
    ids = {}
    waits = []
    state = {"mute": False}

    def sem(*key):
        return ids.setdefault(key, len(ids))

    def load(src, dst):
        copy = pltpu.make_async_copy(src, dst, lsem.at[count["l"]])
        count["l"] += 1
        copy.start()
        return copy

    def copy_of(src, dst, device, index, at=None):
        return pltpu.make_async_remote_copy(
            src_ref=src, dst_ref=dst, send_sem=ssem.at[index],
            recv_sem=rsem.at[index if at is None else at], device_id=device, device_id_type=MESH,
        )

    def send(src, dst, device, index, at=None, like=None, cond=None):
        if not state["mute"]:
            copy_of(src, dst, device, index, at).start()
            waits.append((like or (lambda: src), index, cond))

    def arrived(dst, index):
        copy_of(dst, dst, dev(c_=other), index).wait_recv()

    def dot(a, b):
        return jnp.dot(a, b, preferred_element_type=F32)

    p_load, x_load = {}, []
    for k in (2, 1, 3, 0):
        b = plus(y, k)
        p_load[k] = load(p_hbm.at[:, pl.ds(pl.multiple_of(b * 256, 256), 256)], p_v.at[b])
        if k == 2:
            x_load.append(load(x_hbm, x_v))
    m_load = [load(m1_hbm, m_v.at[0]), load(m2_hbm, m_v.at[1])]
    ct_load = load(ct_hbm, ct_v.at[y])
    w_load = load(w_hbm, w_v)

    barrier = pltpu.get_barrier_semaphore()

    def signal(device):
        pl.semaphore_signal(barrier, inc=1, device_id=device, device_id_type=MESH)

    for k in (1, 2, 3):
        signal(dev(y_=plus(y, k)))
        signal(dev(zl_=plus(zl, k)))
        signal(dev(x_=plus(x, k)))
        signal(dev(zh_=plus(zh, k)))
    signal(dev(c_=other))
    for k in range(4):
        source = plus(x, k)
        signal(dev(x_=source, c_=other, zl_=x))
        if k == 0:

            @pl.when(apart)
            def _():
                signal(dev(zl_=x))
        else:
            signal(dev(x_=source, zl_=x))

    swapped = dev(zh_=y, y_=zh)

    @pl.when(moved)
    def _():
        signal(swapped)

    def enter():
        for far in (True, False):
            for off in (True, False):
                here = (moved if far else jnp.logical_not(moved)) & (apart if off else jnp.logical_not(apart))

                @pl.when(here)
                def _():
                    pl.semaphore_wait(barrier, 20 + far + off)

    def project(k):
        p_load[k].wait()
        return dot(x_v[...], p_v[plus(y, k)]).reshape(4, 2, 64, 256)

    def give_y(k, h, u):
        send(ys.at[k - 1, h, u], yr.at[k - 1, h, u], dev(y_=plus(y, k)), sem("y", k, h, u))

    def m0(_):
        x_load[0].wait()
        for k in (2, 1, 3):
            block = project(k).astype(BF16)
            for h in range(2):
                for u in range(2):
                    ys[k - 1, h, u] = block[:, u, :, h * 128 : h * 128 + 128]
            if k == 2:
                enter()
            for u in range(2):
                give_y(k, 0, u)
        for u in range(2):
            for k in (2, 1, 3):
                give_y(k, 1, u)
        for copy in m_load:
            copy.wait()

        @pl.when(moved)
        def _():
            send(m_v, mr_v, swapped, sem("m"), like=lambda: m_v, cond=lambda: moved)

        @pl.when(jnp.logical_not(moved))
        def _():
            mr_v[...] = m_v[...]

        block = project(0)
        for h in range(2):
            for u in range(2):
                yown[h, u] = block[:, u, :, h * 128 : h * 128 + 128]

    def z1(s):
        h, u = divmod(s, 2)
        total = yown[h, u]
        for k in (1, 3, 2):
            arrived(yr.at[k - 1, h, u], sem("y", k, h, u))
            total = total + yr[k - 1, h, u].astype(F32)
        yown[h, u] = total
        zs[h, u] = total.astype(BF16)
        for k in (2, 1, 3):
            to = plus(zl, k)
            send(zs.at[h, u, to], zr.at[h, u, k - 1], dev(zl_=to), sem("z", k, s))

    def ct(_):
        ct_load.wait()
        for k in (2, 1, 3):
            send(ct_v.at[y], ct_v.at[y], dev(y_=plus(y, k)), sem("ct", k))

    def z2(s):
        h, u = divmod(s, 2)
        total = yown[h, u, zl]
        for k in (1, 2, 3):
            arrived(zr.at[h, u, k - 1], sem("z", k, s))
            total = total + zr[h, u, k - 1].astype(F32)
        proj[h, u, zl] = total.astype(BF16)
        for k in (2, 1, 3):
            send(proj.at[h, u, zl], proj.at[h, u, zl], dev(zl_=plus(zl, k)), sem("za", k, s))

    def dt(s):
        h, u = divmod(s, 2)
        if s == 0:
            for k in (1, 2, 3):
                arrived(ct_v.at[plus(y, 4 - k)], sem("ct", k))
        for k in (1, 2, 3):
            arrived(proj.at[h, u, plus(zl, 4 - k)], sem("za", k, s))
        left = proj[h, u].reshape(256, 128)
        for b in range(4):
            right = jnp.concatenate([ct_v[b, (2 * z + u) * 64 : (2 * z + u) * 64 + 64] for z in range(4)], axis=0)
            block = lax.dot_general(left, right, (((0,), (0,)), ((), ())), preferred_element_type=F32)
            block = block.reshape(2, 2, 32, 256)
            for i in range(2):
                for cc in range(2):
                    if u == 0:
                        plow[h, cc, i, b] = block[i, cc]
                    else:
                        plow[h, cc, i, b] += block[i, cc]
        if u == 1:
            cs[h] = plow[h, other].astype(BF16)
            send(cs.at[h], cr.at[h], dev(c_=other), sem("c", h))

    def bx(h):
        arrived(cr.at[h], sem("c", h))
        total = plow[h, c] + cr[h].astype(F32)
        csum[h] = total
        xs[h] = total.astype(BF16)
        for k in (2, 1, 3):
            to = plus(x, k)

            @pl.when(lax.div(to, 2) == h)
            def _():
                send(
                    xs.at[h, lax.rem(to, 2)], xr.at[k - 1], dev(x_=to), sem("x", k),
                    like=lambda: xs.at[0, 0], cond=lambda k=k: lax.div(plus(x, k), 2) == h,
                )

    def bh(h):
        @pl.when(xh == h)
        def _():
            total = csum[h, xx]
            for k in (1, 3, 2):
                arrived(xr.at[k - 1], sem("x", k))
                total = total + xr[k - 1].astype(F32)
            xsum[...] = total
            hs[...] = total.astype(BF16)
            for k in (2, 1, 3):
                to = plus(zh, k)
                send(
                    hs.at[to], hr.at[k - 1], dev(zh_=to), sem("h", k),
                    like=lambda: hs.at[0], cond=lambda: xh == h,
                )

    def moments(m, low):
        return 0.9 * m[0] + 0.1 * low, 0.999 * m[1] + 0.001 * low * low

    def ad(h):
        @pl.when(moved & (xh == h))
        def _():
            arrived(mr_v, sem("m"))

        @pl.when(xh == h)
        def _():
            total = xsum[zh]
            for k in (1, 3, 2):
                arrived(hr.at[k - 1], sem("h", k))
                total = total + hr[k - 1].astype(F32)
            low = total / REPLICAS
            low_v[...] = low
            first, second = moments(mr_v, low)
            first_hat = first / (1.0 - 0.9**STEP)
            second_hat = second / (1.0 - 0.999**STEP)
            update = (first_hat / (jnp.sqrt(second_hat) + 1e-08)).astype(BF16)
            upd[0] = update[:, :128]
            upd[1] = update[:, 128:]
            place = need.at[y, x, c]
            at = sem("n", 0, 0, 0) + x * 2 + c
            for k in (2, 1, 3, 0):
                for same in (0, 1):
                    half = c if same else other
                    device = dev(x_=zl, c_=half, zl_=plus(zl, k))
                    index = sem("n", 1, k, same)
                    rest = dict(like=lambda: upd.at[0])
                    if k == 0 and same:

                        @pl.when(apart)
                        def _():
                            send(upd.at[c], place, device, index, at, cond=lambda: apart & (xh == h), **rest)

                        @pl.when(jnp.logical_not(apart))
                        def _():
                            need[y, x, c] = upd[c]
                    else:
                        send(upd.at[half], place, device, index, at, cond=lambda: xh == h, **rest)

        @pl.when((xh == h) & moved)
        def _():
            send(low_v, back, swapped, sem("b"), like=lambda: back, cond=lambda: (xh == h) & moved)

    def c1(h):
        for i in (2 * h, 2 * h + 1):
            for cc in range(2):

                @pl.when(jnp.logical_or(apart, jnp.logical_or(i != x, cc != c)))
                def _():
                    arrived(need.at[y, i, cc], sem("n", 0, i, cc))

        mine = need.at[y, pl.ds(2 * h, 2)]
        for k in (2, 1, 3):
            send(mine, mine, dev(y_=plus(y, k)), sem("g", k, h))

    def d(h):
        for k in (1, 3, 2):
            arrived(need.at[plus(y, 4 - k), pl.ds(2 * h, 2)], sem("g", k, h))
        if h == 1:
            w_load.wait()
        lower = [need[a, 2 * h : 2 * h + 2].reshape(128, 128) for a in range(4)]
        for r in range(0, 1024, 256):
            span = slice(r, r + 256)
            change = sum(dot(p_v[a, span, h * 128 : h * 128 + 128], lower[a]) for a in range(4))
            if h == 0:
                acc[span] = change
            else:
                ow[span] = (w_v[span].astype(F32) - 0.5 * (acc[span] + change)).astype(BF16)

    def own(_):
        @pl.when(moved)
        def _():
            arrived(back, sem("b"))

        @pl.when(jnp.logical_not(moved))
        def _():
            back[...] = low_v[...]

        o1[...], o2[...] = moments(m_v, back[...])

    for i in range(4):
        for cc in range(2):
            sem("n", 0, i, cc)
    plan = [
        (0, m0, 0), (4.7, z1, 0), (6.7, z1, 1), (6.8, ct, 0), (8.7, z1, 2), (8.9, z2, 0), (10.7, z1, 3), (10.9, z2, 1),
        (12.9, z2, 2), (14.9, z2, 3), (15.2, dt, 0), (16, dt, 1), (17.1, dt, 2), (17.5, bx, 0), (19.1, dt, 3),
        (20.5, bx, 1), (21.1, bh, 0), (24.5, bh, 1), (28, ad, 0), (32, ad, 1), (33, c1, 0), (37, c1, 1), (38, d, 0), (41, d, 1),
        (42, own, 0),
    ]
    for _, stage, index in plan:
        stage(index)

    for like, index, cond in waits:
        wait = copy_of(like(), like(), dev(c_=other), index).wait_send
        if cond is None:
            wait()
        else:
            pl.when(cond())(wait)


def local(weight, inputs, cotangent, projector, first_moment, second_moment):
    v = pltpu.VMEM
    return pl.pallas_call(
        kernel,
        out_shape=(
            jax.ShapeDtypeStruct((1024, 128), BF16),
            jax.ShapeDtypeStruct((32, 256), F32),
            jax.ShapeDtypeStruct((32, 256), F32),
        ),
        in_specs=[pl.BlockSpec(memory_space=pl.ANY)] * 6,
        out_specs=[pl.BlockSpec(memory_space=pltpu.VMEM)] * 3,
        scratch_shapes=[
            v((1024, 128), BF16),
            v((512, 1024), BF16),
            v((4, 512, 256), BF16),
            v((4, 1024, 256), BF16),
            v((2, 32, 256), F32),
            v((2, 32, 256), F32),
            v((3, 2, 2, 4, 64, 128), BF16),
            v((3, 2, 2, 4, 64, 128), BF16),
            v((2, 2, 4, 64, 128), F32),
            v((2, 2, 4, 64, 128), BF16),
            v((2, 2, 3, 64, 128), BF16),
            v((2, 2, 4, 64, 128), BF16),
            v((2, 2, 2, 4, 32, 256), F32),
            v((2, 2, 4, 32, 256), BF16),
            v((2, 2, 4, 32, 256), BF16),
            v((2, 2, 4, 32, 256), F32),
            v((2, 2, 4, 32, 256), BF16),
            v((3, 4, 32, 256), BF16),
            v((4, 32, 256), F32),
            v((4, 32, 256), BF16),
            v((3, 32, 256), BF16),
            v((32, 256), F32),
            v((32, 256), F32),
            v((2, 32, 128), BF16),
            v((4, 4, 2, 32, 128), BF16),
            v((1024, 128), F32),
            pltpu.SemaphoreType.DMA((20,)),
            pltpu.SemaphoreType.DMA((96,)),
            pltpu.SemaphoreType.DMA((96,)),
        ],
        compiler_params=pltpu.CompilerParams(
            collective_id=0, has_side_effects=True, vmem_limit_bytes=58 * 2**20
        ),
    )(weight, inputs, cotangent, projector, first_moment, second_moment)


def solution(mesh):
    placed = (
        P("tensor", "dp"),
        P("dp", "tensor"),
        P("dp", "tensor"),
        P("tensor", None),
        P("dp", "tensor"),
        P("dp", "tensor"),
    )
    return jax.shard_map(
        local,
        mesh=mesh,
        in_specs=placed,
        out_specs=(P("tensor", "dp"), P("dp", "tensor"), P("dp", "tensor")),
        check_vma=False,
    )
```

time: 425 us -> 73.1 us (0.17)
  waiting for transfers between devices: 261 us -> 0 us
  blocking collectives: 138 us -> 0 us
  Pallas kernels: 0 us -> 67.7 us
  between operations: 14.1 us -> 0.64 us
  matrix products: 7.04 us -> 0 us
    all_gather x1 -> x0, waiting for transfers between devices: 137 us -> none  [local(): lax.all_gather(group_rows, 'dp', axis=0, tiled=True)]
    reduce_scatter x1 -> x0, waiting for transfers between devices: 124 us -> none  [local(): lax.psum_scatter(partial_low, 'dp', scatter_dimension=0, tiled=True)]
    psum x1 -> x0, blocking collectives: 101 us -> none  [local(): projected = lax.psum(partial_proj, 'tensor').astype(jnp.bfloat16)]
    pallas_call x0 -> x1, Pallas kernels: none -> 67.7 us  [local(): pl.pallas_call(kernel, out_shape=(jax.ShapeDtypeStruct((1024, 128), BF16)...]
    all_gather x1 -> x0, blocking collectives: 37 us -> none  [local(): group_rows = lax.all_gather(update, 'tensor', axis=1, tiled=True)]
    dot_general x3 -> x0, matrix products: 7.04 us -> none  [the longest x1 3.82 us: local(): jnp.dot(inputs, projector, preferred_element_type=jnp.float32)]
  transfers between devices with their start and end apart: 2 -> 0, of which waited for: 2 -> 0; matrix products, arithmetic and copies ran while one was open for 0% -> 0% of each run, Pallas kernels for 0% -> 0%
where the time goes in v2:
time: 73.1 us; the launch traced here: 72.8 us
  Pallas kernels  67.7 us (93%)
  local copies, waits for them, and re-layouts  4.42 us (6%)
    pallas_call x1, Pallas kernels, local(): pl.pallas_call(kernel, out_shape=(jax.ShapeDtypeStruct((1024, 128), BF16)...  67.7 us
    unnamed x3, local copies, waits for them, and re-layouts  4.42 us

profile of v2, /device:TPU:1, one launch (start us, length us, event | category | flops | bytes accessed | tf_op | source)
XLA Modules:
  0.0 72.8 jit_solution(5953366546544094538)
XLA Ops:
  0.6 67.7 %shard_map.85 = (bf16[1024,128]{1,0:T(8,128)(2,1)}, f32[32,256]{1,0:T(8,128)}, f32[32,256]{1,0:T(8,128)}) custom-call(bf16[1024,128]{1,0:T(8,128)(2,1)} %w_hbm.1, bf16[512,1024]{1,0:T(8,128)(2,1)} %x_hbm.1, bf16[512,256]{1,0:T(8,128)(2,1)} %ct_hbm.1, bf16[1024,1024]{1,0:T(8,128)(2,1)} %p_hbm.1, f32[32,256]{1,0:T(8,128)} %m1_hbm.1, f32[32,256]{1,0:T(8,128)} %m2_hbm.1), custom_call_target="tpu_custom_call" | custom-call | tf_op jit(solution)/shard_map/pallas_call | solution.py:336
  68.3 1.7 %copy.12 = bf16[1024,128]{1,0:T(8,128)(2,1)} copy(bf16[1024,128]{1,0:T(8,128)(2,1)} %get-tuple-element.6) | data formatting | bytes 524288
  70.0 1.4 %copy.13 = f32[32,256]{1,0:T(8,128)} copy(f32[32,256]{1,0:T(8,128)} %get-tuple-element.7) | data formatting | bytes 65536
  71.4 1.4 %copy.14 = f32[32,256]{1,0:T(8,128)} copy(f32[32,256]{1,0:T(8,128)} %get-tuple-element.8) | data formatting | bytes 65536

commit v3 on v2

--- a/solution.py
+++ b/solution.py
@@ -15,9 +15,9 @@
     w_hbm, x_hbm, ct_hbm, p_hbm, m1_hbm, m2_hbm,
     ow, o1, o2,
     w_v, x_v, ct_v, p_v, m_v, mr_v,
-    ys, yr, yown, zs, zr, proj,
+    y1s, y1r, y2s, y2r, mid, yown, zs, zr, proj,
     plow, cs, cr, csum, xs, xr, xsum, hs, hr, low_v, back, upd, need, acc,
-    lsem, ssem, rsem,
+    lsem, ssem, rsem, known,
 ):
     dp, t = lax.axis_index("dp"), lax.axis_index("tensor")
     zh, x, c = lax.div(dp, 8), lax.rem(lax.div(dp, 2), 4), lax.rem(dp, 2)
@@ -79,81 +79,88 @@
     def signal(device):
         pl.semaphore_signal(barrier, inc=1, device_id=device, device_id_type=MESH)
 
-    for k in (1, 2, 3):
-        signal(dev(y_=plus(y, k)))
-        signal(dev(zl_=plus(zl, k)))
-        signal(dev(x_=plus(x, k)))
-        signal(dev(zh_=plus(zh, k)))
-    signal(dev(c_=other))
-    for k in range(4):
-        source = plus(x, k)
-        signal(dev(x_=source, c_=other, zl_=x))
-        if k == 0:
-
-            @pl.when(apart)
-            def _():
-                signal(dev(zl_=x))
-        else:
-            signal(dev(x_=source, zl_=x))
-
     swapped = dev(zh_=y, y_=zh)
-
-    @pl.when(moved)
-    def _():
-        signal(swapped)
+    around = [dev(zh_=plus(zh, k)) for k in (1, 3)]
+    y_up, y_down = dev(y_=plus(y, 1)), dev(y_=plus(y, 3))
+    near = [y_up, y_down, dev(c_=other)]
+    near += [dev(zl_=plus(zl, k)) for k in (1, 2, 3)]
+    near += [dev(x_=plus(x, k)) for k in (1, 2, 3)]
+    near += around
+    for device in near:
+        signal(device)
 
     def enter():
-        for far in (True, False):
-            for off in (True, False):
-                here = (moved if far else jnp.logical_not(moved)) & (apart if off else jnp.logical_not(apart))
-
-                @pl.when(here)
-                def _():
-                    pl.semaphore_wait(barrier, 20 + far + off)
+        pl.semaphore_wait(barrier, len(near))
+        spread(0)
+
+    def spread(step):
+        for i in range(2):
+            pl.semaphore_signal(known.at[step, i], inc=1, device_id=around[i], device_id_type=MESH)
+
+    def heard(step):
+        for i in range(2):
+            pl.semaphore_wait(known.at[step, i], 1)
 
     def project(k):
         p_load[k].wait()
         return dot(x_v[...], p_v[plus(y, k)]).reshape(4, 2, 64, 256)
 
-    def give_y(k, h, u):
-        send(ys.at[k - 1, h, u], yr.at[k - 1, h, u], dev(y_=plus(y, k)), sem("y", k, h, u))
+    def cut(block, h, u):
+        return block[:, u, :, h * 128 : h * 128 + 128]
 
     def m0(_):
         x_load[0].wait()
-        for k in (2, 1, 3):
-            block = project(k).astype(BF16)
+        block = project(2).astype(BF16)
+        for h in range(2):
+            for u in range(2):
+                y1s[h, u] = cut(block, h, u)
+        enter()
+        for h in range(2):
+            for u in range(2):
+                send(y1s.at[h, u, pl.ds(0, 2)], y1r.at[0, h, u], y_up, sem("y1", 0, h, u))
+                send(y1s.at[h, u, pl.ds(2, 2)], y1r.at[1, h, u], y_down, sem("y1", 1, h, u))
+        for i, k in enumerate((1, 3)):
+            block = project(k)
             for h in range(2):
                 for u in range(2):
-                    ys[k - 1, h, u] = block[:, u, :, h * 128 : h * 128 + 128]
-            if k == 2:
-                enter()
-            for u in range(2):
-                give_y(k, 0, u)
-        for u in range(2):
-            for k in (2, 1, 3):
-                give_y(k, 1, u)
-        for copy in m_load:
-            copy.wait()
-
-        @pl.when(moved)
-        def _():
-            send(m_v, mr_v, swapped, sem("m"), like=lambda: m_v, cond=lambda: moved)
-
-        @pl.when(jnp.logical_not(moved))
-        def _():
-            mr_v[...] = m_v[...]
-
+                    mid[i, h, u] = cut(block, h, u)
         block = project(0)
         for h in range(2):
             for u in range(2):
-                yown[h, u] = block[:, u, :, h * 128 : h * 128 + 128]
+                yown[h, u] = cut(block, h, u)
+
+    def y1(s):
+        h, u = divmod(s, 2)
+        for i, device in enumerate((y_up, y_down)):
+            added, rest = (pl.ds(0, 2), pl.ds(2, 2)) if i == 0 else (pl.ds(2, 2), pl.ds(0, 2))
+            y2s[i, h, u, rest] = mid[i, h, u, rest].astype(BF16)
+            arrived(y1r.at[i, h, u], sem("y1", i, h, u))
+            y2s[i, h, u, added] = (mid[i, h, u, added] + y1r[i, h, u].astype(F32)).astype(BF16)
+            send(y2s.at[i, h, u], y2r.at[i, h, u], device, sem("y2", i, h, u))
+
+    def hop(_):
+        heard(0)
+        spread(1)
+
+    def mo(_):
+        heard(1)
+        for copy in m_load:
+            copy.wait()
+
+        @pl.when(moved)
+        def _():
+            send(m_v, mr_v, swapped, sem("m"), like=lambda: m_v, cond=lambda: moved)
+
+        @pl.when(jnp.logical_not(moved))
+        def _():
+            mr_v[...] = m_v[...]
 
     def z1(s):
         h, u = divmod(s, 2)
         total = yown[h, u]
-        for k in (1, 3, 2):
-            arrived(yr.at[k - 1, h, u], sem("y", k, h, u))
-            total = total + yr[k - 1, h, u].astype(F32)
+        for i in range(2):
+            arrived(y2r.at[i, h, u], sem("y2", i, h, u))
+            total = total + y2r[i, h, u].astype(F32)
         yown[h, u] = total
         zs[h, u] = total.astype(BF16)
         for k in (2, 1, 3):
@@ -162,8 +169,17 @@
 
     def ct(_):
         ct_load.wait()
-        for k in (2, 1, 3):
-            send(ct_v.at[y], ct_v.at[y], dev(y_=plus(y, k)), sem("ct", k))
+        send(ct_v.at[y], ct_v.at[y], y_up, sem("ct", 0))
+        send(ct_v.at[y], ct_v.at[y], y_down, sem("ct", 1))
+
+    def cf(_):
+        up, down = plus(y, 3), plus(y, 1)
+        arrived(ct_v.at[up], sem("ct", 0))
+        first = ct_v.at[up, pl.ds(0, 256)]
+        send(first, first, y_up, sem("cf", 0))
+        arrived(ct_v.at[down], sem("ct", 1))
+        second = ct_v.at[down, pl.ds(256, 256)]
+        send(second, second, y_down, sem("cf", 1))
 
     def z2(s):
         h, u = divmod(s, 2)
@@ -178,8 +194,8 @@
     def dt(s):
         h, u = divmod(s, 2)
         if s == 0:
-            for k in (1, 2, 3):
-                arrived(ct_v.at[plus(y, 4 - k)], sem("ct", k))
+            arrived(ct_v.at[plus(y, 2), pl.ds(0, 256)], sem("cf", 0))
+            arrived(ct_v.at[plus(y, 2), pl.ds(256, 256)], sem("cf", 1))
         for k in (1, 2, 3):
             arrived(proj.at[h, u, plus(zl, 4 - k)], sem("za", k, s))
         left = proj[h, u].reshape(256, 128)
@@ -314,13 +330,13 @@
     for i in range(4):
         for cc in range(2):
             sem("n", 0, i, cc)
-    plan = [
-        (0, m0, 0), (4.7, z1, 0), (6.7, z1, 1), (6.8, ct, 0), (8.7, z1, 2), (8.9, z2, 0), (10.7, z1, 3), (10.9, z2, 1),
-        (12.9, z2, 2), (14.9, z2, 3), (15.2, dt, 0), (16, dt, 1), (17.1, dt, 2), (17.5, bx, 0), (19.1, dt, 3),
-        (20.5, bx, 1), (21.1, bh, 0), (24.5, bh, 1), (28, ad, 0), (32, ad, 1), (33, c1, 0), (37, c1, 1), (38, d, 0), (41, d, 1),
-        (42, own, 0),
-    ]
-    for _, stage, index in plan:
+    plan = [(m0, 0)] + [(y1, s) for s in range(4)]
+    plan += [(z1, 0), (z1, 1), (ct, 0), (z1, 2), (z1, 3)]
+    plan += [(z2, s) for s in range(4)] + [(hop, 0), (cf, 0)] + [(dt, s) for s in range(4)]
+    plan += [(bx, 0), (bx, 1), (mo, 0)]
+    plan += [(stage, h) for stage in (bh, ad, c1, d) for h in range(2)]
+    plan += [(own, 0)]
+    for stage, index in plan:
         stage(index)
 
     for like, index, cond in waits:
@@ -331,15 +347,22 @@
             pl.when(cond())(wait)
 
 
+def leave(a, b, c, oa, ob, oc):
+    oa[...] = a[...]
+    ob[...] = b[...]
+    oc[...] = c[...]
+
+
 def local(weight, inputs, cotangent, projector, first_moment, second_moment):
     v = pltpu.VMEM
-    return pl.pallas_call(
+    shapes = (
+        jax.ShapeDtypeStruct((1024, 128), BF16),
+        jax.ShapeDtypeStruct((32, 256), F32),
+        jax.ShapeDtypeStruct((32, 256), F32),
+    )
+    results = pl.pallas_call(
         kernel,
-        out_shape=(
-            jax.ShapeDtypeStruct((1024, 128), BF16),
-            jax.ShapeDtypeStruct((32, 256), F32),
-            jax.ShapeDtypeStruct((32, 256), F32),
-        ),
+        out_shape=shapes,
         in_specs=[pl.BlockSpec(memory_space=pl.ANY)] * 6,
         out_specs=[pl.BlockSpec(memory_space=pltpu.VMEM)] * 3,
         scratch_shapes=[
@@ -349,8 +372,11 @@
             v((4, 1024, 256), BF16),
             v((2, 32, 256), F32),
             v((2, 32, 256), F32),
-            v((3, 2, 2, 4, 64, 128), BF16),
-            v((3, 2, 2, 4, 64, 128), BF16),
+            v((2, 2, 4, 64, 128), BF16),
+            v((2, 2, 2, 2, 64, 128), BF16),
+            v((2, 2, 2, 4, 64, 128), BF16),
+            v((2, 2, 2, 4, 64, 128), BF16),
+            v((2, 2, 2, 4, 64, 128), F32),
             v((2, 2, 4, 64, 128), F32),
             v((2, 2, 4, 64, 128), BF16),
             v((2, 2, 3, 64, 128), BF16),
@@ -372,11 +398,19 @@
             pltpu.SemaphoreType.DMA((20,)),
             pltpu.SemaphoreType.DMA((96,)),
             pltpu.SemaphoreType.DMA((96,)),
+            pltpu.SemaphoreType.REGULAR((2, 2)),
         ],
         compiler_params=pltpu.CompilerParams(
             collective_id=0, has_side_effects=True, vmem_limit_bytes=58 * 2**20
         ),
     )(weight, inputs, cotangent, projector, first_moment, second_moment)
+    return pl.pallas_call(
+        leave,
+        out_shape=shapes,
+        in_specs=[pl.BlockSpec(memory_space=pltpu.VMEM)] * 3,
+        out_specs=[pl.BlockSpec(memory_space=pltpu.VMEM)] * 3,
+        compiler_params=pltpu.CompilerParams(vmem_limit_bytes=58 * 2**20),
+    )(*results)
 
 
 def solution(mesh):

time: 73.1 us -> 67.1 us (0.918)
  the two profiles are of different devices: /device:TPU:1 before, /device:TPU:6 now
where the time goes in v3:
time: 67.1 us; the launch traced here: 66.9 us
  Pallas kernels  66.3 us (99%)
    pallas_call x1, Pallas kernels, local(): pl.pallas_call(kernel, out_shape=shapes, in_specs=[pl.BlockSpec(memory_sp...  64.6 us
    pallas_call x1, Pallas kernels, local(): pl.pallas_call(leave, out_shape=shapes, in_specs=[pl.BlockSpec(memory_spa...  1.7 us

profile of v3, /device:TPU:6, one launch (start us, length us, event | category | flops | bytes accessed | tf_op | source)
XLA Modules:
  0.0 66.9 jit_solution(18192834266741703314)
XLA Ops:
  0.6 64.6 %shard_map.85 = (bf16[1024,128]{1,0:T(8,128)(2,1)}, f32[32,256]{1,0:T(8,128)}, f32[32,256]{1,0:T(8,128)}) custom-call(bf16[1024,128]{1,0:T(8,128)(2,1)} %w_hbm.1, bf16[512,1024]{1,0:T(8,128)(2,1)} %x_hbm.1, bf16[512,256]{1,0:T(8,128)(2,1)} %ct_hbm.1, bf16[1024,1024]{1,0:T(8,128)(2,1)} %p_hbm.1, f32[32,256]{1,0:T(8,128)} %m1_hbm.1, f32[32,256]{1,0:T(8,128)} %m2_hbm.1), custom_call_target="tpu_custom_call" | custom-call | tf_op jit(solution)/shard_map/pallas_call | solution.py:363
  65.2 1.7 %shard_map.86 = (bf16[1024,128]{1,0:T(8,128)(2,1)}, f32[32,256]{1,0:T(8,128)}, f32[32,256]{1,0:T(8,128)}) custom-call(bf16[1024,128]{1,0:T(8,128)(2,1)} %get-tuple-element.6.a, f32[32,256]{1,0:T(8,128)} %get-tuple-element.7.b, f32[32,256]{1,0:T(8,128)} %get-tuple-element.8.c), custom_call_target="tpu_custom_call" | custom-call | tf_op jit(solution)/shard_map/pallas_call | solution.py:407

commit v4 on v3

--- a/solution.py
+++ b/solution.py
@@ -64,6 +64,21 @@
     def dot(a, b):
         return jnp.dot(a, b, preferred_element_type=F32)
 
+    barrier = pltpu.get_barrier_semaphore()
+
+    def signal(device):
+        pl.semaphore_signal(barrier, inc=1, device_id=device, device_id_type=MESH)
+
+    swapped = dev(zh_=y, y_=zh)
+    around = [dev(zh_=plus(zh, k)) for k in (1, 3)]
+    y_up, y_down = dev(y_=plus(y, 1)), dev(y_=plus(y, 3))
+    near = [y_up, y_down, dev(c_=other)]
+    near += [dev(zl_=plus(zl, k)) for k in (1, 2, 3)]
+    near += [dev(x_=plus(x, k)) for k in (1, 2, 3)]
+    near += around
+    for device in near:
+        signal(device)
+
     p_load, x_load = {}, []
     for k in (2, 1, 3, 0):
         b = plus(y, k)
@@ -73,21 +88,6 @@
     m_load = [load(m1_hbm, m_v.at[0]), load(m2_hbm, m_v.at[1])]
     ct_load = load(ct_hbm, ct_v.at[y])
     w_load = load(w_hbm, w_v)
-
-    barrier = pltpu.get_barrier_semaphore()
-
-    def signal(device):
-        pl.semaphore_signal(barrier, inc=1, device_id=device, device_id_type=MESH)
-
-    swapped = dev(zh_=y, y_=zh)
-    around = [dev(zh_=plus(zh, k)) for k in (1, 3)]
-    y_up, y_down = dev(y_=plus(y, 1)), dev(y_=plus(y, 3))
-    near = [y_up, y_down, dev(c_=other)]
-    near += [dev(zl_=plus(zl, k)) for k in (1, 2, 3)]
-    near += [dev(x_=plus(x, k)) for k in (1, 2, 3)]
-    near += around
-    for device in near:
-        signal(device)
 
     def enter():
         pl.semaphore_wait(barrier, len(near))
@@ -167,19 +167,22 @@
             to = plus(zl, k)
             send(zs.at[h, u, to], zr.at[h, u, k - 1], dev(zl_=to), sem("z", k, s))
 
-    def ct(_):
+    def ca(_):
         ct_load.wait()
-        send(ct_v.at[y], ct_v.at[y], y_up, sem("ct", 0))
-        send(ct_v.at[y], ct_v.at[y], y_down, sem("ct", 1))
+        for i, device in enumerate((y_up, y_down)):
+            part = ct_v.at[y, pl.ds(i * 256, 256)]
+            send(part, part, device, sem("ca", i))
+
+    def cb(_):
+        for i, device in enumerate((y_up, y_down)):
+            part = ct_v.at[y, pl.ds(256 - i * 256, 256)]
+            send(part, part, device, sem("cb", i))
 
     def cf(_):
-        up, down = plus(y, 3), plus(y, 1)
-        arrived(ct_v.at[up], sem("ct", 0))
-        first = ct_v.at[up, pl.ds(0, 256)]
-        send(first, first, y_up, sem("cf", 0))
-        arrived(ct_v.at[down], sem("ct", 1))
-        second = ct_v.at[down, pl.ds(256, 256)]
-        send(second, second, y_down, sem("cf", 1))
+        for i, device in enumerate((y_up, y_down)):
+            part = ct_v.at[plus(y, 3 - 2 * i), pl.ds(i * 256, 256)]
+            arrived(part, sem("ca", i))
+            send(part, part, device, sem("cf", i))
 
     def z2(s):
         h, u = divmod(s, 2)
@@ -194,8 +197,9 @@
     def dt(s):
         h, u = divmod(s, 2)
         if s == 0:
-            arrived(ct_v.at[plus(y, 2), pl.ds(0, 256)], sem("cf", 0))
-            arrived(ct_v.at[plus(y, 2), pl.ds(256, 256)], sem("cf", 1))
+            for i in range(2):
+                arrived(ct_v.at[plus(y, 3 - 2 * i), pl.ds(256 - i * 256, 256)], sem("cb", i))
+                arrived(ct_v.at[plus(y, 2), pl.ds(i * 256, 256)], sem("cf", i))
         for k in (1, 2, 3):
             arrived(proj.at[h, u, plus(zl, 4 - k)], sem("za", k, s))
         left = proj[h, u].reshape(256, 128)
@@ -331,11 +335,11 @@
         for cc in range(2):
             sem("n", 0, i, cc)
     plan = [(m0, 0)] + [(y1, s) for s in range(4)]
-    plan += [(z1, 0), (z1, 1), (ct, 0), (z1, 2), (z1, 3)]
-    plan += [(z2, s) for s in range(4)] + [(hop, 0), (cf, 0)] + [(dt, s) for s in range(4)]
-    plan += [(bx, 0), (bx, 1), (mo, 0)]
+    plan += [(z1, 0), (ca, 0), (z1, 1), (cb, 0), (z1, 2), (z1, 3), (hop, 0), (cf, 0)]
+    plan += [(z2, s) for s in range(4)] + [(dt, s) for s in range(4)] + [(mo, 0), (bx, 0), (bx, 1)]
     plan += [(stage, h) for stage in (bh, ad, c1, d) for h in range(2)]
     plan += [(own, 0)]
+
     for stage, index in plan:
         stage(index)
 

time: 67.1 us -> 62.8 us (0.936)
  the two profiles are of different devices: /device:TPU:6 before, /device:TPU:1 now
where the time goes in v4:
time: 62.8 us; the launch traced here: 62.6 us
  Pallas kernels  62 us (99%)
  between operations  0.64 us (1%)
    pallas_call x1, Pallas kernels, local(): pl.pallas_call(kernel, out_shape=shapes, in_specs=[pl.BlockSpec(memory_sp...  60.3 us
    pallas_call x1, Pallas kernels, local(): pl.pallas_call(leave, out_shape=shapes, in_specs=[pl.BlockSpec(memory_spa...  1.7 us

profile of v4, /device:TPU:1, one launch (start us, length us, event | category | flops | bytes accessed | tf_op | source)
XLA Modules:
  0.0 62.6 jit_solution(9807042626155061987)
XLA Ops:
  0.6 60.3 %shard_map.85 = (bf16[1024,128]{1,0:T(8,128)(2,1)}, f32[32,256]{1,0:T(8,128)}, f32[32,256]{1,0:T(8,128)}) custom-call(bf16[1024,128]{1,0:T(8,128)(2,1)} %w_hbm.1, bf16[512,1024]{1,0:T(8,128)(2,1)} %x_hbm.1, bf16[512,256]{1,0:T(8,128)(2,1)} %ct_hbm.1, bf16[1024,1024]{1,0:T(8,128)(2,1)} %p_hbm.1, f32[32,256]{1,0:T(8,128)} %m1_hbm.1, f32[32,256]{1,0:T(8,128)} %m2_hbm.1), custom_call_target="tpu_custom_call" | custom-call | tf_op jit(solution)/shard_map/pallas_call | solution.py:367
  60.9 1.7 %shard_map.86 = (bf16[1024,128]{1,0:T(8,128)(2,1)}, f32[32,256]{1,0:T(8,128)}, f32[32,256]{1,0:T(8,128)}) custom-call(bf16[1024,128]{1,0:T(8,128)(2,1)} %get-tuple-element.6.a, f32[32,256]{1,0:T(8,128)} %get-tuple-element.7.b, f32[32,256]{1,0:T(8,128)} %get-tuple-element.8.c), custom_call_target="tpu_custom_call" | custom-call | tf_op jit(solution)/shard_map/pallas_call | solution.py:411

commit v5 on v4

--- a/solution.py
+++ b/solution.py
@@ -16,7 +16,7 @@
     ow, o1, o2,
     w_v, x_v, ct_v, p_v, m_v, mr_v,
     y1s, y1r, y2s, y2r, mid, yown, zs, zr, proj,
-    plow, cs, cr, csum, xs, xr, xsum, hs, hr, low_v, back, upd, need, acc,
+    plow, cs, cr, csum, xs, xr, xsum, hs, hr, low_v, back, upd, need, acc, nw_v, nm_v,
     lsem, ssem, rsem, known,
 ):
     dp, t = lax.axis_index("dp"), lax.axis_index("tensor")
@@ -36,6 +36,7 @@
     count = {"l": 0}
     ids = {}
     waits = []
+    leaving = []
     state = {"mute": False}
 
     def sem(*key):
@@ -318,7 +319,8 @@
             if h == 0:
                 acc[span] = change
             else:
-                ow[span] = (w_v[span].astype(F32) - 0.5 * (acc[span] + change)).astype(BF16)
+                nw_v[span] = (w_v[span].astype(F32) - 0.5 * (acc[span] + change)).astype(BF16)
+                leaving.append(load(nw_v.at[pl.ds(r, 256)], ow.at[pl.ds(r, 256)]))
 
     def own(_):
         @pl.when(moved)
@@ -329,7 +331,9 @@
         def _():
             back[...] = low_v[...]
 
-        o1[...], o2[...] = moments(m_v, back[...])
+        nm_v[0], nm_v[1] = moments(m_v, back[...])
+        leaving.append(load(nm_v.at[0], o1))
+        leaving.append(load(nm_v.at[1], o2))
 
     for i in range(4):
         for cc in range(2):
@@ -343,6 +347,8 @@
     for stage, index in plan:
         stage(index)
 
+    for copy in leaving:
+        copy.wait()
     for like, index, cond in waits:
         wait = copy_of(like(), like(), dev(c_=other), index).wait_send
         if cond is None:
@@ -368,7 +374,7 @@
         kernel,
         out_shape=shapes,
         in_specs=[pl.BlockSpec(memory_space=pl.ANY)] * 6,
-        out_specs=[pl.BlockSpec(memory_space=pltpu.VMEM)] * 3,
+        out_specs=[pl.BlockSpec(memory_space=pl.ANY)] * 3,
         scratch_shapes=[
             v((1024, 128), BF16),
             v((512, 1024), BF16),
@@ -399,6 +405,8 @@
             v((2, 32, 128), BF16),
             v((4, 4, 2, 32, 128), BF16),
             v((1024, 128), F32),
+            v((1024, 128), BF16),
+            v((2, 32, 256), F32),
             pltpu.SemaphoreType.DMA((20,)),
             pltpu.SemaphoreType.DMA((96,)),
             pltpu.SemaphoreType.DMA((96,)),

time: 62.8 us -> 62.7 us (level)
  no operation moved by 1% of the time
where the time goes in v5:
time: 62.7 us; the launch traced here: 62.6 us
  Pallas kernels  61.9 us (99%)
  between operations  0.64 us (1%)
    pallas_call x1, Pallas kernels, local(): pl.pallas_call(kernel, out_shape=shapes, in_specs=[pl.BlockSpec(memory_sp...  60.2 us
    pallas_call x1, Pallas kernels, local(): pl.pallas_call(leave, out_shape=shapes, in_specs=[pl.BlockSpec(memory_spa...  1.7 us

profile of v5, /device:TPU:1, one launch (start us, length us, event | category | flops | bytes accessed | tf_op | source)
XLA Modules:
  0.0 62.6 jit_solution(2600093104974282487)
XLA Ops:
  0.6 60.2 %shard_map.85 = (bf16[1024,128]{1,0:T(8,128)(2,1)}, f32[32,256]{1,0:T(8,128)}, f32[32,256]{1,0:T(8,128)}) custom-call(bf16[1024,128]{1,0:T(8,128)(2,1)} %w_hbm.1, bf16[512,1024]{1,0:T(8,128)(2,1)} %x_hbm.1, bf16[512,256]{1,0:T(8,128)(2,1)} %ct_hbm.1, bf16[1024,1024]{1,0:T(8,128)(2,1)} %p_hbm.1, f32[32,256]{1,0:T(8,128)} %m1_hbm.1, f32[32,256]{1,0:T(8,128)} %m2_hbm.1), custom_call_target="tpu_custom_call" | custom-call | tf_op jit(solution)/shard_map/pallas_call | solution.py:373
  60.9 1.7 %shard_map.86 = (bf16[1024,128]{1,0:T(8,128)(2,1)}, f32[32,256]{1,0:T(8,128)}, f32[32,256]{1,0:T(8,128)}) custom-call(bf16[1024,128]{1,0:T(8,128)(2,1)} %get-tuple-element.6.a, f32[32,256]{1,0:T(8,128)} %get-tuple-element.7.b, f32[32,256]{1,0:T(8,128)} %get-tuple-element.8.c), custom_call_target="tpu_custom_call" | custom-call | tf_op jit(solution)/shard_map/pallas_call | solution.py:419
